TPU v7x, 256 devices: a whole 4x4x8 slice. The times are simulated.
256 devices in a mesh: pair: 2 (over core), rep: 32 (over z, x), slab: 4 (over y).
Axes of the slice: x: 4, y: 4, z: 8, core: 2. Of those that a mesh axis runs over, the one named last changes fastest.
Arguments:
- amplitudes: bfloat16 [16384, 4096], P(('pair', 'slab'), 'rep'), may hold values from -6 to 6
- tile_pairs: int32 [16384], P(('pair', 'slab')), may hold values from 0 to 15, as said below
- row_pairs: int32 [16384], P(('pair', 'slab')), may hold values from 0 to 255
- owner: int32 [16], replicated, may hold values from 0 to 15, as said below
- integrals: bfloat16 [2, 16, 4096, 4096], P(None, 'pair', 'rep', 'slab'), may hold values from -0.0625 to 0.0625
Outputs:
- ladder: bfloat16 [2048, 2, 4096], P(('pair', 'slab'), None, 'rep')
Inputs may be any that keep to these rules, and one draw needn't show every extreme that they name: Each occupied pair of a device is named by exactly 8 of its rows, with distinct tile pairs. Call slots p * 8 to (p + 1) * 8 - 1 owner block p. At most 6 tiles of one occupied pair have slots owner[tile_pairs] in one owner block; in the rows of one device at most 1536 do, and every device reaches 1536 for some block. `owner`: each value once.
All inputs are finite; a program needn't handle non-finite values.
Results may differ from a plain program's by a relative error of at most 0.001.
Values may be sent and summed in bfloat16 or wider, within the bound.
No kernel may reach another device: no remote copies, remote signals or barrier semaphores. Data moves between devices by JAX's collectives and lax.ppermute only.
A program may use at most 128 MiB of HBM per device.

v0:
```python
import jax
import jax.numpy as jnp
from jax import lax
from jax.sharding import PartitionSpec as P

PAIRS_DEV = 256


def body(amplitudes, tile_pairs, row_pairs, owner, integrals):
    groups = lax.axis_size("pair")
    tile_count = owner.shape[0]
    slot_width = tile_count // groups
    part_width = amplitudes.shape[1]
    lookup = tile_pairs[:, None] == jnp.arange(tile_count, dtype=jnp.int32)[None, :]
    slots = jnp.sum(jnp.where(lookup, owner[None, :], 0), axis=1)
    target = slots // slot_width
    local_slot = slots % slot_width
    place = (target * PAIRS_DEV + row_pairs) * slot_width + local_slot
    sendbuf = (
        jnp.zeros((groups * PAIRS_DEV * slot_width, part_width), jnp.bfloat16)
        .at[place]
        .set(amplitudes)
    )
    received = lax.all_to_all(
        sendbuf.reshape(groups, PAIRS_DEV * slot_width, part_width),
        "pair",
        split_axis=0,
        concat_axis=0,
        tiled=True,
    )
    operand = received.reshape(groups * PAIRS_DEV, slot_width * part_width)
    piece = lax.all_gather(integrals, "slab", axis=3, tiled=True)
    flat_piece = piece.reshape(piece.shape[0], -1, piece.shape[3])
    products = jnp.einsum("rk,ckn->rcn", operand, flat_piece, preferred_element_type=jnp.float32)
    partial_sum = lax.psum_scatter(products, "rep", scatter_dimension=2, tiled=True)
    result = lax.psum_scatter(partial_sum, "pair", scatter_dimension=0, tiled=True)
    return result.astype(jnp.bfloat16)


def solution(mesh):
    return jax.shard_map(
        body,
        mesh=mesh,
        in_specs=(
            P(("pair", "slab"), "rep"),
            P(("pair", "slab")),
            P(("pair", "slab")),
            P(),
            P(None, "pair", "rep", "slab"),
        ),
        out_specs=P(("pair", "slab"), None, "rep"),
        check_vma=False,
    )
```

profile of v0, /device:TPU:1, one launch (start us, length us, event | category | flops | bytes accessed | tf_op | source)
XLA Modules:
  0.0 454.6 jit_solution(795973035956883995)
XLA Ops:
  6.5 0.0 all-gather.2.cloned.1.call-start
  6.5 0.7 all-gather.2.cloned.1.call-update
  7.3 0.0 reduce-scatter.3.cloned.1.call-start
  7.3 0.8 select_reduce_fusion
  8.1 0.7 compare_select_fusion
  8.8 6.4 %scatter_custom_fusion = bf16[4096,128]{1,0:T(8,128)(2,1)S(1)} fusion(s32[2048]{0:T(1024)S(1)} %compare_select_fusion, bf16[2048,128]{1,0:T(8,128)(2,1)} %param.5, bf16[]{:T(256)} %constant.28.clone.1), kind=kCustom, calls=%fused_computation.1 | custom fusion | bytes 1049088 | tf_op jit(solution)/shard_map/scatter | solution.py:22
  15.2 7.4 %all_to_all.5 = bf16[2,2048,128]{2,1,0:T(8,128)(2,1)S(1)} all-to-all(bf16[2,2048,128]{2,1,0:T(8,128)(2,1)S(1)} %bitcast.5), channel_id=1, replica_groups=mesh['pair'=2,'rep'=32,'slab'=4] {'pair'}, dimensions={0} | all-to-all | bytes 2097152 | tf_op jit(solution)/shard_map/all_to_all | solution.py:24
  22.7 0.5 reshape.23
  23.2 146.4 %all-gather.2.cloned.1.call-done = bf16[2,8,128,4096]{3,2,1,0:T(8,128)(2,1)} async-done(((bf16[2,8,128,1024]{3,2,1,0:T(8,128)(2,1)}), bf16[2,8,128,4096]{3,2,1,0:T(8,128)(2,1)}) %all-gather.2.cloned.1.call-update) | async-done | bytes 16777232 | tf_op jit(solution)/shard_map/all_gather | solution.py:32
  169.6 15.6 %fusion.10 = f32[512,2,4096]{2,0,1:T(8,128)} fusion(bf16[512,1024,1]{1,0,2:T(8,128)(2,1)S(1)} %reshape.23, bf16[2,1024,4096]{2,1,0:T(8,128)(2,1)} %bitcast.6), kind=kOutput, calls=%fused_computation.20 | convolution fusion | flops 8589934592 | bytes 34603008 | tf_op jit(solution)/shard_map/rk,ckn->rcn/dot_general | solution.py:34
  185.2 0.0 reduce-scatter.3.cloned.1.call-update
  185.2 0.0 reduce-scatter.5.cloned.1.call-start
  185.3 242.3 %reduce-scatter.3.cloned.1.call-done = f32[512,2,128]{2,0,1:T(8,128)} async-done(((f32[512,2,4096]{2,0,1:T(8,128)}), f32[512,2,128]{2,0,1:T(8,128)}) %reduce-scatter.3.cloned.1.call-update) | async-done | bytes 524304 | tf_op jit(solution)/shard_map/reduce_scatter | solution.py:35
  427.6 0.0 reduce-scatter.5.cloned.1.call-update
  427.6 18.7 %reduce-scatter.5.cloned.1.call-done = f32[256,2,128]{2,0,1:T(8,128)} async-done(((f32[512,2,128]{2,0,1:T(8,128)}), f32[256,2,128]{2,0,1:T(8,128)}) %reduce-scatter.5.cloned.1.call-update) | async-done | bytes 262160 | tf_op jit(solution)/shard_map/reduce_scatter | solution.py:36
  446.3 1.0 convert_element_type.3
  447.2 0.8 copy.8
Async XLA Ops:
  6.5 163.1 %all-gather.2.cloned.1.call-start = ((), (), s32[]{:S(2)}) async-start(), calls=%async_computation.3 | async-start | bytes 20971520 | tf_op jit(solution)/shard_map/all_gather | solution.py:32
  7.3 420.3 %reduce-scatter.3.cloned.1.call-start = ((), (), s32[]{:S(2)}) async-start(), calls=%async_computation.4 | async-start | bytes 17301504 | tf_op jit(solution)/shard_map/reduce_scatter | solution.py:35
  185.2 261.0 %reduce-scatter.5.cloned.1.call-start = ((), (), s32[]{:S(2)}) async-start(), calls=%async_computation.5 | async-start | bytes 786432 | tf_op jit(solution)/shard_map/reduce_scatter | solution.py:36
Sparse Core Ops, SparseCore 0:
  9.2 160.4 all-gather.1
  185.4 242.1 reduce-scatter.2
  430.1 16.1 reduce-scatter.4
where the time goes:
time: 455 us
  waiting for transfers between devices  408 us (90%)
  matrix products  15.6 us (3%)
  between operations  13.1 us (3%)
  local copies, waits for them, and re-layouts  7.67 us (2%)
  blocking collectives  7.44 us (2%)
    reduce_scatter x1, waiting for transfers between devices, body(): lax.psum_scatter(products, 'rep', scatter_dimension=2, tiled=True)  242 us
    all_gather x1, waiting for transfers between devices, body(): piece = lax.all_gather(integrals, 'slab', axis=3, tiled=True)  146 us
    reduce_scatter x1, waiting for transfers between devices, body(): lax.psum_scatter(partial_sum, 'pair', scatter_dimension=0, tiled=True)  18.7 us
    dot_general x1, matrix products, body(): jnp.einsum('rk,ckn->rcn', operand, flat_piece, preferred_element_type=jnp...  15.6 us
  transfers between devices with their start and end apart: 3, of which 3 were waited for; matrix products, arithmetic and copies ran while one was open for 2% of the time, Pallas kernels for 0%

commit v1 on v0

--- a/solution.py
+++ b/solution.py
@@ -29,7 +29,9 @@
         tiled=True,
     )
     operand = received.reshape(groups * PAIRS_DEV, slot_width * part_width)
-    piece = lax.all_gather(integrals, "slab", axis=3, tiled=True)
+    piece = jnp.concatenate(
+        lax.all_to_all(jnp.stack([integrals] * lax.axis_size("slab")), "slab", 0, 0), axis=3
+    )
     flat_piece = piece.reshape(piece.shape[0], -1, piece.shape[3])
     products = jnp.einsum("rk,ckn->rcn", operand, flat_piece, preferred_element_type=jnp.float32)
     partial_sum = lax.psum_scatter(products, "rep", scatter_dimension=2, tiled=True)

time: 455 us -> 556 us (1.22)
  local copies, waits for them, and re-layouts: 7.67 us -> 64.9 us
  waiting for transfers between devices: 408 us -> 444 us
  starting transfers between devices: 0.08 us -> 7.04 us
    all_to_all x0 -> x1, waiting for transfers between devices: none -> 183 us  [body(): lax.all_to_all(jnp.stack([integrals] * lax.axis_size('slab')), 'slab', 0, 0)]
    all_gather x1 -> x0, waiting for transfers between devices: 146 us -> none  [body(): piece = lax.all_gather(integrals, 'slab', axis=3, tiled=True)]
    another operation x0 -> x2, local copies, waits for them, and re-layouts: none -> 35 us  [the longest x1 27.6 us: body(): flat_piece = piece.reshape(piece.shape[0], -1, piece.shape[3])]
    reshape x0 -> x1, local copies, waits for them, and re-layouts: none -> 22.2 us  [body(): jnp.concatenate(lax.all_to_all(jnp.stack([integrals] * lax.axis_size('sla...]
    all_to_all x0 -> x1, starting transfers between devices: none -> 6.96 us  [body(): lax.all_to_all(jnp.stack([integrals] * lax.axis_size('slab')), 'slab', 0, 0)]
  transfers between devices with their start and end apart: 3 -> 3, of which waited for: 3 -> 3; matrix products, arithmetic and copies ran while one was open for 2% -> 0% of each run, Pallas kernels for 0% -> 0%
where the time goes in v1:
time: 556 us; the launch traced here: 555 us
  waiting for transfers between devices  444 us (80%)
  local copies, waits for them, and re-layouts  64.9 us (12%)
  matrix products  15.6 us (3%)
  between operations  13.4 us (2%)
  blocking collectives  7.44 us (1%)
  starting transfers between devices  7.04 us (1%)
    reduce_scatter x1, waiting for transfers between devices, body(): lax.psum_scatter(products, 'rep', scatter_dimension=2, tiled=True)  242 us
    all_to_all x1, waiting for transfers between devices, body(): lax.all_to_all(jnp.stack([integrals] * lax.axis_size('slab')), 'slab', 0, 0)  183 us
    another operation x1, local copies, waits for them, and re-layouts, body(): flat_piece = piece.reshape(piece.shape[0], -1, piece.shape[3])  27.6 us
    reshape x1, local copies, waits for them, and re-layouts, body(): jnp.concatenate(lax.all_to_all(jnp.stack([integrals] * lax.axis_size('sla...  22.2 us
    reduce_scatter x1, waiting for transfers between devices, body(): lax.psum_scatter(partial_sum, 'pair', scatter_dimension=0, tiled=True)  19 us
    dot_general x1, matrix products, body(): jnp.einsum('rk,ckn->rcn', operand, flat_piece, preferred_element_type=jnp...  15.6 us
  transfers between devices with their start and end apart: 3, of which 3 were waited for; matrix products, arithmetic and copies ran while one was open for 0% of the time, Pallas kernels for 0%

profile of v1, /device:TPU:1, one launch (start us, length us, event | category | flops | bytes accessed | tf_op | source)
XLA Modules:
  0.0 554.6 jit_solution(14287037318151042676)
XLA Ops:
  6.5 0.8 select_reduce_fusion
  7.3 0.7 compare_select_fusion
  8.1 6.4 %scatter_custom_fusion = bf16[4096,128]{1,0:T(8,128)(2,1)S(1)} fusion(s32[2048]{0:T(1024)S(1)} %compare_select_fusion, bf16[2048,128]{1,0:T(8,128)(2,1)} %param.5, bf16[]{:T(256)} %constant.28.clone.1), kind=kCustom, calls=%fused_computation.1 | custom fusion | bytes 1049088 | tf_op jit(solution)/shard_map/scatter | solution.py:22
  14.5 7.4 %all_to_all.10 = bf16[2,2048,128]{2,1,0:T(8,128)(2,1)S(1)} all-to-all(bf16[2,2048,128]{2,1,0:T(8,128)(2,1)S(1)} %bitcast.4), channel_id=1, replica_groups=mesh['pair'=2,'rep'=32,'slab'=4] {'pair'}, dimensions={0} | all-to-all | bytes 2097152 | tf_op jit(solution)/shard_map/all_to_all | solution.py:24
  21.9 7.5 %stack.2 = bf16[4,2,8,128,1024]{4,3,2,1,0:T(8,128)(2,1)} broadcast(bf16[2,8,128,1024]{3,2,1,0:T(8,128)(2,1)} %param.9), dimensions={1,2,3,4} | broadcast | bytes 20971520 | tf_op jit(solution)/shard_map/stack | solution.py:33
  29.4 7.0 %all-to-all-start.1 = ((bf16[4,2,8,128,1024]{4,3,2,1,0:T(8,128)(2,1)}), bf16[4,2,8,128,1024]{4,3,2,1,0:T(8,128)(2,1)}, u32[]{:S(2)}, u32[]{:S(2)}) async-start(bf16[4,2,8,128,1024]{4,3,2,1,0:T(8,128)(2,1)} %stack.2), calls=%async_computation.1 | async-start | bytes 33554432 | tf_op jit(solution)/shard_map/all_to_all | solution.py:33
  36.3 0.0 reduce-scatter.3.cloned.1.call-start
  36.4 0.5 reshape.25
  36.9 182.9 %all-to-all-done.1 = bf16[4,2,8,128,1024]{4,3,2,1,0:T(8,128)(2,1)} async-done(((bf16[4,2,8,128,1024]{4,3,2,1,0:T(8,128)(2,1)}), bf16[4,2,8,128,1024]{4,3,2,1,0:T(8,128)(2,1)}, u32[]{:S(2)}, u32[]{:S(2)}) %all-to-all-start.1) | async-done | bytes 16777248 | tf_op jit(solution)/shard_map/all_to_all | solution.py:33
  219.8 22.2 %copy.10 = bf16[2,8,128,4,1024]{4,3,2,1,0:T(4,128)(2,1)} copy(bf16[2,8,128,4,1024]{4,2,1,0,3:T(8,128)(2,1)} %bitcast.1) | data formatting | bytes 33554432 | tf_op jit(solution)/shard_map/reshape | solution.py:32
  242.0 27.6 %reshape_reshape.3 = bf16[2,1024,4096]{2,1,0:T(8,128)(2,1)} reshape(bf16[2,8,128,4,1024]{4,3,2,1,0:T(4,128)(2,1)} %copy.10) | data formatting | bytes 33554432 | tf_op jit(solution)/shard_map/reshape;reshape | solution.py:35
  269.5 15.6 %fusion.10 = f32[512,2,4096]{2,0,1:T(8,128)} fusion(bf16[512,1024,1]{1,0,2:T(8,128)(2,1)S(1)} %reshape.25, bf16[2,1024,4096]{2,1,0:T(8,128)(2,1)} %reshape_reshape.3), kind=kOutput, calls=%fused_computation.20 | convolution fusion | flops 8589934592 | bytes 34603008 | tf_op jit(solution)/shard_map/rk,ckn->rcn/dot_general | solution.py:36
  285.1 0.0 reduce-scatter.3.cloned.1.call-update
  285.2 0.0 reduce-scatter.5.cloned.1.call-start
  285.2 241.7 %reduce-scatter.3.cloned.1.call-done = f32[512,2,128]{2,0,1:T(8,128)} async-done(((f32[512,2,4096]{2,0,1:T(8,128)}), f32[512,2,128]{2,0,1:T(8,128)}) %reduce-scatter.3.cloned.1.call-update) | async-done | bytes 524304 | tf_op jit(solution)/shard_map/reduce_scatter | solution.py:37
  526.9 0.0 reduce-scatter.5.cloned.1.call-update
  526.9 19.0 %reduce-scatter.5.cloned.1.call-done = f32[256,2,128]{2,0,1:T(8,128)} async-done(((f32[512,2,128]{2,0,1:T(8,128)}), f32[256,2,128]{2,0,1:T(8,128)}) %reduce-scatter.5.cloned.1.call-update) | async-done | bytes 262160 | tf_op jit(solution)/shard_map/reduce_scatter | solution.py:38
  546.0 1.0 convert_element_type.3
  546.9 0.8 copy.11
Async XLA Ops:
  29.4 190.4 %all-to-all-start.1 = ((bf16[4,2,8,128,1024]{4,3,2,1,0:T(8,128)(2,1)}), bf16[4,2,8,128,1024]{4,3,2,1,0:T(8,128)(2,1)}, u32[]{:S(2)}, u32[]{:S(2)}) async-start(bf16[4,2,8,128,1024]{4,3,2,1,0:T(8,128)(2,1)} %stack.2), calls=%async_computation.1 | async-start | bytes 33554432 | tf_op jit(solution)/shard_map/all_to_all | solution.py:33
  36.3 490.5 %reduce-scatter.3.cloned.1.call-start = ((), (), s32[]{:S(2)}) async-start(), calls=%async_computation.4 | async-start | bytes 17301504 | tf_op jit(solution)/shard_map/reduce_scatter | solution.py:37
  285.2 260.8 %reduce-scatter.5.cloned.1.call-start = ((), (), s32[]{:S(2)}) async-start(), calls=%async_computation.5 | async-start | bytes 786432 | tf_op jit(solution)/shard_map/reduce_scatter | solution.py:38
Sparse Core Ops, SparseCore 0:
  285.3 241.5 reduce-scatter.2
  529.4 16.5 reduce-scatter.4
